TPU v7x, 1024 devices: a whole 4x4x32 slice. The times are simulated.
1024 devices in a mesh: row: 256 (over y, z, core), col: 4 (over x).
Axes of the slice: x: 4, y: 4, z: 32, core: 2. Of those that a mesh axis runs over, the one named last changes fastest.
Arguments:
- a_tiles: bfloat16 [4096, 8, 128, 128], P('row', 'col'), may hold values from -0.5 to 0.5
- a_cols: int32 [4096, 8], P('row', 'col'), may hold values from 0 to 4095, as said below
- p_tiles: bfloat16 [4096, 3, 128, 128], P('row'), may hold values from -0.5 to 0.5
- p_cols: int32 [4096, 3], replicated, may hold values from 0 to 1023, as said below
- c_cols: int32 [1024, 8], replicated, may hold values from 0 to 1023, as said below
Outputs:
- coarse: float32 [1024, 8, 128, 128], P('row', None, 'col')
Inputs may be any that keep to these rules, and one draw needn't show every extreme that they name: `a_cols`: a row's entries are distinct and lie within 8 of the row's own index. `p_cols`: a row's entries are distinct and lie within 2 of the row's index times 4 // 16. `c_cols`: a row's entries are distinct and lie within 8 of the row's own index.
All inputs are finite; a program needn't handle non-finite values.
Results may differ from a plain program's by a relative error of at most 0.0029.
Values may be sent and summed in bfloat16 or wider, within the bound.
A program may use at most 32 MiB of HBM per device.

v0:
```python
import jax
import jax.numpy as jnp
from jax import lax
from jax.sharding import PartitionSpec as P


def padded(block, sides, width):
    for axis, dim in sides:
        count = lax.axis_size(axis)
        forward = [(i, i + 1) for i in range(count - 1)]
        backward = [(target, source) for source, target in forward]
        low = lax.ppermute(
            lax.slice_in_dim(block, block.shape[dim] - width, None, axis=dim), axis, forward
        )
        high = lax.ppermute(lax.slice_in_dim(block, 0, width, axis=dim), axis, backward)
        block = jnp.concatenate([low, block, high], axis=dim)
    return block


def passed_along(block, axis, distance):
    devices = range(lax.axis_size(axis))
    route = [(i - distance, i) for i in devices if i - distance in devices]
    return lax.ppermute(block, axis, route)


def per_device(a_tiles, a_cols, p_tiles, p_cols, c_cols):
    rows_here = a_tiles.shape[0]
    width = a_tiles.shape[2]
    col_count = lax.axis_size("col")
    reach = a_tiles.shape[1] * col_count
    coarse_here = c_cols.shape[0] // lax.axis_size("row")
    pattern_len = c_cols.shape[1]
    owner = lax.axis_index("row")
    first_fine = owner * rows_here
    first_coarse = (owner - 1) * coarse_here
    dummy = 3 * coarse_here * pattern_len
    slot_ids = jnp.arange(pattern_len, dtype=jnp.int32)
    extended = padded(p_tiles, (("row", 0),), reach)

    def step(acc, local_row):
        tiles = a_tiles[local_row]
        interp = p_tiles[local_row]
        left = jnp.einsum(
            "pkx,aky->paxy", interp, tiles, preferred_element_type=jnp.float32
        ).astype(jnp.bfloat16)
        columns = a_cols[local_row]
        remote = extended[columns - first_fine + reach]
        term = jnp.einsum("paxk,aqky->paqxy", left, remote, preferred_element_type=jnp.float32)
        coarse_i = p_cols[first_fine + local_row]
        coarse_j = p_cols[columns]
        pattern = c_cols[coarse_i]
        match = pattern[:, None, None, :] == coarse_j[None, :, :, None]
        found = jnp.any(match, axis=-1)
        slot = jnp.sum(jnp.where(match, slot_ids, 0), axis=-1)
        target = (coarse_i - first_coarse)[:, None, None] * pattern_len + slot
        flat = jnp.where(found, target, dummy)
        acc = acc.at[flat.reshape(-1)].add(term.reshape(-1, width, width), mode="drop")
        return (acc, None)

    start = jnp.zeros((dummy, width, width), jnp.float32)
    acc, _ = lax.scan(step, start, jnp.arange(rows_here, dtype=jnp.int32))
    blocks = acc.reshape(3, coarse_here * pattern_len, width, width)
    received = blocks[1]
    for shift_by, portion in ((-1, blocks[0]), (1, blocks[2])):
        received = received + passed_along(portion, "row", shift_by)
    total = lax.psum_scatter(received, "col", scatter_dimension=1, tiled=True)
    return total.reshape(coarse_here, pattern_len, width // col_count, width)


def solution(mesh):
    in_specs = (P("row", "col", None, None), P("row", "col"), P("row", None, None, None), P(), P())
    out_specs = P("row", None, "col", None)
    return jax.shard_map(
        per_device, mesh=mesh, in_specs=in_specs, out_specs=out_specs, check_vma=False
    )
```

profile of v0, /device:TPU:24, one launch (start us, length us, event | category | flops | bytes accessed | tf_op | source)
XLA Modules:
  0.0 452.4 jit_solution(321685172311587115)
XLA Ops:
  10.0 18.3 %collective-permute-start.1 = (bf16[8,3,128,128]{3,2,1,0:T(8,128)(2,1)S(1)}, bf16[8,3,128,128]{3,2,1,0:T(8,128)(2,1)S(1)}, u32[]{:S(2)}, u32[]{:S(2)}) collective-permute-start(bf16[8,3,128,128]{3,2,1,0:T(8,128)(2,1)S(1)} %get-tuple-element.241), channel_id=1, source_target_pairs={{4,0},{8,4},{12,8},{16,12},{20,16},{24,20},{28,24},{32,28},{36,32}... | collective-permute-start | bytes 2359304 | tf_op jit(solution)/shard_map/ppermute | solution.py:15
  31.4 4.7 %collective-permute-done = bf16[8,3,128,128]{3,2,1,0:T(8,128)(2,1)S(1)} collective-permute-done((bf16[8,3,128,128]{3,2,1,0:T(8,128)(2,1)S(1)}, bf16[8,3,128,128]{3,2,1,0:T(8,128)(2,1)S(1)}, u32[]{:S(2)}, u32[]{:S(2)}) %collective-permute-start) | collective-permute-done | bytes 786464 | tf_op jit(solution)/shard_map/ppermute | solution.py:12
  37.8 3.0 pad_maximum_fusion
  40.8 3.4 broadcast_in_dim.30
  44.2 320.0 %while.13 = (s32[]{:T(128)}, f32[96,128,128]{2,1,0:T(8,128)}, s32[16]{0:T(128)S(1)}, s32[]{:T(128)}, s32[4096,3]{1,0:T(8,128)}, /*index=5*/s32[1024,8]{1,0:T(8,1...) while((s32[]{:T(128)}, f32[96,128,128]{2,1,0:T(8,128)}, ...), condition=%wide.region_4.5_spmd.clone, body=%wide.region_0.4_spmd.clone.sunk | while | flops 101060400 | bytes 7846585 | solution.py:61
  50.4 2.1 gather_fusion
  53.7 2.5 gather_fusion.2
  58.0 6.2 %scatter_fusion = f32[96,128,128]{2,1,0:T(8,128)} fusion(f32[96,128,128]{2,1,0:T(8,128)} %get-tuple-element.333, s32[18]{0:T(128)S(1)} %fusion.35, f32[18,128,128]{2,1,0:T(8,128)S(1)} %bitcast.75), kind=kCustom, calls=%fused_computation.3.clone.clone.1 | custom fusion | flops 294912 | bytes 3539016 | tf_op jit(solution)/shard_map/while/body/eval_jaxpr/scatter-add | solution.py:57
  70.4 2.1 gather_fusion
  73.7 2.5 gather_fusion.2
  78.0 6.2 %scatter_fusion = f32[96,128,128]{2,1,0:T(8,128)} fusion(f32[96,128,128]{2,1,0:T(8,128)} %get-tuple-element.333, s32[18]{0:T(128)S(1)} %fusion.35, f32[18,128,128]{2,1,0:T(8,128)S(1)} %bitcast.75), kind=kCustom, calls=%fused_computation.3.clone.clone.1 | custom fusion | flops 294912 | bytes 3539016 | tf_op jit(solution)/shard_map/while/body/eval_jaxpr/scatter-add | solution.py:57
  90.4 2.1 gather_fusion
  93.7 2.5 gather_fusion.2
  98.0 6.3 %scatter_fusion = f32[96,128,128]{2,1,0:T(8,128)} fusion(f32[96,128,128]{2,1,0:T(8,128)} %get-tuple-element.333, s32[18]{0:T(128)S(1)} %fusion.35, f32[18,128,128]{2,1,0:T(8,128)S(1)} %bitcast.75), kind=kCustom, calls=%fused_computation.3.clone.clone.1 | custom fusion | flops 294912 | bytes 3539016 | tf_op jit(solution)/shard_map/while/body/eval_jaxpr/scatter-add | solution.py:57
  110.4 2.1 gather_fusion
  113.7 2.5 gather_fusion.2
  118.0 6.2 %scatter_fusion = f32[96,128,128]{2,1,0:T(8,128)} fusion(f32[96,128,128]{2,1,0:T(8,128)} %get-tuple-element.333, s32[18]{0:T(128)S(1)} %fusion.35, f32[18,128,128]{2,1,0:T(8,128)S(1)} %bitcast.75), kind=kCustom, calls=%fused_computation.3.clone.clone.1 | custom fusion | flops 294912 | bytes 3539016 | tf_op jit(solution)/shard_map/while/body/eval_jaxpr/scatter-add | solution.py:57
  130.4 2.1 gather_fusion
  133.7 2.5 gather_fusion.2
  138.0 6.2 %scatter_fusion = f32[96,128,128]{2,1,0:T(8,128)} fusion(f32[96,128,128]{2,1,0:T(8,128)} %get-tuple-element.333, s32[18]{0:T(128)S(1)} %fusion.35, f32[18,128,128]{2,1,0:T(8,128)S(1)} %bitcast.75), kind=kCustom, calls=%fused_computation.3.clone.clone.1 | custom fusion | flops 294912 | bytes 3539016 | tf_op jit(solution)/shard_map/while/body/eval_jaxpr/scatter-add | solution.py:57
  153.7 2.5 gather_fusion.2
  158.0 6.3 %scatter_fusion = f32[96,128,128]{2,1,0:T(8,128)} fusion(f32[96,128,128]{2,1,0:T(8,128)} %get-tuple-element.333, s32[18]{0:T(128)S(1)} %fusion.35, f32[18,128,128]{2,1,0:T(8,128)S(1)} %bitcast.75), kind=kCustom, calls=%fused_computation.3.clone.clone.1 | custom fusion | flops 294912 | bytes 3539016 | tf_op jit(solution)/shard_map/while/body/eval_jaxpr/scatter-add | solution.py:57
  173.8 2.5 gather_fusion.2
  178.1 6.2 %scatter_fusion = f32[96,128,128]{2,1,0:T(8,128)} fusion(f32[96,128,128]{2,1,0:T(8,128)} %get-tuple-element.333, s32[18]{0:T(128)S(1)} %fusion.35, f32[18,128,128]{2,1,0:T(8,128)S(1)} %bitcast.75), kind=kCustom, calls=%fused_computation.3.clone.clone.1 | custom fusion | flops 294912 | bytes 3539016 | tf_op jit(solution)/shard_map/while/body/eval_jaxpr/scatter-add | solution.py:57
  193.7 2.5 gather_fusion.2
  198.1 6.2 %scatter_fusion = f32[96,128,128]{2,1,0:T(8,128)} fusion(f32[96,128,128]{2,1,0:T(8,128)} %get-tuple-element.333, s32[18]{0:T(128)S(1)} %fusion.35, f32[18,128,128]{2,1,0:T(8,128)S(1)} %bitcast.75), kind=kCustom, calls=%fused_computation.3.clone.clone.1 | custom fusion | flops 294912 | bytes 3539016 | tf_op jit(solution)/shard_map/while/body/eval_jaxpr/scatter-add | solution.py:57
  213.7 2.5 gather_fusion.2
  218.0 6.2 %scatter_fusion = f32[96,128,128]{2,1,0:T(8,128)} fusion(f32[96,128,128]{2,1,0:T(8,128)} %get-tuple-element.333, s32[18]{0:T(128)S(1)} %fusion.35, f32[18,128,128]{2,1,0:T(8,128)S(1)} %bitcast.75), kind=kCustom, calls=%fused_computation.3.clone.clone.1 | custom fusion | flops 294912 | bytes 3539016 | tf_op jit(solution)/shard_map/while/body/eval_jaxpr/scatter-add | solution.py:57
  233.7 2.5 gather_fusion.2
  238.0 6.3 %scatter_fusion = f32[96,128,128]{2,1,0:T(8,128)} fusion(f32[96,128,128]{2,1,0:T(8,128)} %get-tuple-element.333, s32[18]{0:T(128)S(1)} %fusion.35, f32[18,128,128]{2,1,0:T(8,128)S(1)} %bitcast.75), kind=kCustom, calls=%fused_computation.3.clone.clone.1 | custom fusion | flops 294912 | bytes 3539016 | tf_op jit(solution)/shard_map/while/body/eval_jaxpr/scatter-add | solution.py:57
  253.8 2.5 gather_fusion.2
  258.1 6.2 %scatter_fusion = f32[96,128,128]{2,1,0:T(8,128)} fusion(f32[96,128,128]{2,1,0:T(8,128)} %get-tuple-element.333, s32[18]{0:T(128)S(1)} %fusion.35, f32[18,128,128]{2,1,0:T(8,128)S(1)} %bitcast.75), kind=kCustom, calls=%fused_computation.3.clone.clone.1 | custom fusion | flops 294912 | bytes 3539016 | tf_op jit(solution)/shard_map/while/body/eval_jaxpr/scatter-add | solution.py:57
  273.8 2.5 gather_fusion.2
  278.1 6.3 %scatter_fusion = f32[96,128,128]{2,1,0:T(8,128)} fusion(f32[96,128,128]{2,1,0:T(8,128)} %get-tuple-element.333, s32[18]{0:T(128)S(1)} %fusion.35, f32[18,128,128]{2,1,0:T(8,128)S(1)} %bitcast.75), kind=kCustom, calls=%fused_computation.3.clone.clone.1 | custom fusion | flops 294912 | bytes 3539016 | tf_op jit(solution)/shard_map/while/body/eval_jaxpr/scatter-add | solution.py:57
  293.8 2.5 gather_fusion.2
  298.1 6.2 %scatter_fusion = f32[96,128,128]{2,1,0:T(8,128)} fusion(f32[96,128,128]{2,1,0:T(8,128)} %get-tuple-element.333, s32[18]{0:T(128)S(1)} %fusion.35, f32[18,128,128]{2,1,0:T(8,128)S(1)} %bitcast.75), kind=kCustom, calls=%fused_computation.3.clone.clone.1 | custom fusion | flops 294912 | bytes 3539016 | tf_op jit(solution)/shard_map/while/body/eval_jaxpr/scatter-add | solution.py:57
  313.8 2.5 gather_fusion.2
  318.1 6.2 %scatter_fusion = f32[96,128,128]{2,1,0:T(8,128)} fusion(f32[96,128,128]{2,1,0:T(8,128)} %get-tuple-element.333, s32[18]{0:T(128)S(1)} %fusion.35, f32[18,128,128]{2,1,0:T(8,128)S(1)} %bitcast.75), kind=kCustom, calls=%fused_computation.3.clone.clone.1 | custom fusion | flops 294912 | bytes 3539016 | tf_op jit(solution)/shard_map/while/body/eval_jaxpr/scatter-add | solution.py:57
  333.8 2.5 gather_fusion.2
  338.1 6.2 %scatter_fusion = f32[96,128,128]{2,1,0:T(8,128)} fusion(f32[96,128,128]{2,1,0:T(8,128)} %get-tuple-element.333, s32[18]{0:T(128)S(1)} %fusion.35, f32[18,128,128]{2,1,0:T(8,128)S(1)} %bitcast.75), kind=kCustom, calls=%fused_computation.3.clone.clone.1 | custom fusion | flops 294912 | bytes 3539016 | tf_op jit(solution)/shard_map/while/body/eval_jaxpr/scatter-add | solution.py:57
  353.7 2.5 gather_fusion.2
  358.1 6.2 %scatter_fusion = f32[96,128,128]{2,1,0:T(8,128)} fusion(f32[96,128,128]{2,1,0:T(8,128)} %get-tuple-element.333, s32[18]{0:T(128)S(1)} %fusion.35, f32[18,128,128]{2,1,0:T(8,128)S(1)} %bitcast.75), kind=kCustom, calls=%fused_computation.3.clone.clone.1 | custom fusion | flops 294912 | bytes 3539016 | tf_op jit(solution)/shard_map/while/body/eval_jaxpr/scatter-add | solution.py:57
  364.3 2.5 fusion.20
  366.8 6.6 %collective-permute-start.2 = (f32[32,128,128]{2,1,0:T(8,128)S(1)}, f32[32,128,128]{2,1,0:T(8,128)S(1)}, u32[]{:S(2)}, u32[]{:S(2)}) collective-permute-start(f32[32,128,128]{2,1,0:T(8,128)S(1)} %get-tuple-element.238), channel_id=1, source_target_pairs={{4,0},{8,4},{12,8},{16,12},{20,16},{24,20},{28,24},{32,28},{36,32}... | collective-permute-start | bytes 6291464 | tf_op jit(solution)/shard_map/ppermute | solution.py:23
  375.3 21.6 %collective-permute-done.2 = f32[32,128,128]{2,1,0:T(8,128)S(1)} collective-permute-done((f32[32,128,128]{2,1,0:T(8,128)S(1)}, f32[32,128,128]{2,1,0:T(8,128)S(1)}, u32[]{:S(2)}, u32[]{:S(2)}) %collective-permute-start.2) | collective-permute-done | bytes 2097184 | tf_op jit(solution)/shard_map/ppermute | solution.py:23
  396.9 5.9 %collective-permute-done.3 = f32[32,128,128]{2,1,0:T(8,128)S(1)} collective-permute-done((f32[32,128,128]{2,1,0:T(8,128)S(1)}, f32[32,128,128]{2,1,0:T(8,128)S(1)}, u32[]{:S(2)}, u32[]{:S(2)}) %collective-permute-start.3) | collective-permute-done | bytes 2097184 | tf_op jit(solution)/shard_map/ppermute | solution.py:23
  402.8 3.4 add_add_fusion
  406.3 39.3 %reduce-scatter.2.cloned.1.call-done = f32[32,32,128]{2,1,0:T(8,128)} async-done(((f32[32,128,128]{2,1,0:T(8,128)}), f32[32,32,128]{2,1,0:T(8,128)}) %reduce-scatter.2.cloned.1.call-update) | async-done | bytes 524304 | tf_op jit(solution)/shard_map/reduce_scatter | solution.py:66
  (299 shorter events, 138.6 us)
Async XLA Ops:
  6.5 21.8 %copy-start.2 = (s32[16,2]{0,1:T(2,128)S(1)}, s32[16,2]{0,1:T(2,128)}, u32[]{:S(2)}) copy-start(s32[16,2]{0,1:T(2,128)} %param.8) | copy-start | bytes 388
  6.5 21.9 %copy-start.1 = (s32[1024,8]{0,1:T(8,128)S(1)}, s32[1024,8]{0,1:T(8,128)}, u32[]{:S(2)}) copy-start(s32[1024,8]{0,1:T(8,128)} %param.11) | copy-start | bytes 98308
  6.5 22.9 %copy-start = (s32[4096,3]{0,1:T(4,128)S(1)}, s32[4096,3]{0,1:T(4,128)}, u32[]{:S(2)}) copy-start(s32[4096,3]{0,1:T(4,128)} %param.10) | copy-start | bytes 147460
  6.5 439.1 %reduce-scatter.2.cloned.1.call-start = ((), (), s32[]{:S(2)}) async-start(), calls=%async_computation.1 | async-start | bytes 2621440 | tf_op jit(solution)/shard_map/reduce_scatter | solution.py:66
  8.1 28.0 %collective-permute-start = (bf16[8,3,128,128]{3,2,1,0:T(8,128)(2,1)S(1)}, bf16[8,3,128,128]{3,2,1,0:T(8,128)(2,1)S(1)}, u32[]{:S(2)}, u32[]{:S(2)}) collective-permute-start(bf16[8,3,128,128]{3,2,1,0:T(8,128)(2,1)S(1)} %get-tuple-element.240), channel_id=1, source_target_pairs={{0,4},{4,8},{8,12},{12,16},{16,20},{20,24},{24,28},{28,32},{32,36}... | collective-permute-start | bytes 2359304 | tf_op jit(solution)/shard_map/ppermute | solution.py:12
  10.0 27.8 %collective-permute-start.1 = (bf16[8,3,128,128]{3,2,1,0:T(8,128)(2,1)S(1)}, bf16[8,3,128,128]{3,2,1,0:T(8,128)(2,1)S(1)}, u32[]{:S(2)}, u32[]{:S(2)}) collective-permute-start(bf16[8,3,128,128]{3,2,1,0:T(8,128)(2,1)S(1)} %get-tuple-element.241), channel_id=1, source_target_pairs={{4,0},{8,4},{12,8},{16,12},{20,16},{24,20},{28,24},{32,28},{36,32}... | collective-permute-start | bytes 2359304 | tf_op jit(solution)/shard_map/ppermute | solution.py:15
  366.8 30.1 %collective-permute-start.2 = (f32[32,128,128]{2,1,0:T(8,128)S(1)}, f32[32,128,128]{2,1,0:T(8,128)S(1)}, u32[]{:S(2)}, u32[]{:S(2)}) collective-permute-start(f32[32,128,128]{2,1,0:T(8,128)S(1)} %get-tuple-element.238), channel_id=1, source_target_pairs={{4,0},{8,4},{12,8},{16,12},{20,16},{24,20},{28,24},{32,28},{36,32}... | collective-permute-start | bytes 6291464 | tf_op jit(solution)/shard_map/ppermute | solution.py:23
  373.3 29.5 %collective-permute-start.3 = (f32[32,128,128]{2,1,0:T(8,128)S(1)}, f32[32,128,128]{2,1,0:T(8,128)S(1)}, u32[]{:S(2)}, u32[]{:S(2)}) collective-permute-start(f32[32,128,128]{2,1,0:T(8,128)S(1)} %get-tuple-element.239), channel_id=1, source_target_pairs={{0,4},{4,8},{8,12},{12,16},{16,20},{20,24},{24,28},{28,32},{32,36}... | collective-permute-start | bytes 6291464 | tf_op jit(solution)/shard_map/ppermute | solution.py:23
Sparse Core Ops, SparseCore 0:
  406.4 39.1 reduce-scatter.1
where the time goes:
time: 460 us; the launch traced here: 452 us
  other arithmetic  140 us (30%)
  local copies, waits for them, and re-layouts  132 us (29%)
  waiting for transfers between devices  73.3 us (16%)
  loops' own time  41.5 us (9%)
  starting transfers between devices  28.7 us (6%)
  matrix products  23.2 us (5%)
  between operations  13.4 us (3%)
    scatter-add x16, other arithmetic, step(): acc.at[flat.reshape(-1)].add(term.reshape(-1, width, width), mode='drop')  99.7 us
    another operation x1, loops' own time, per_device(): acc, _ = lax.scan(step, start, jnp.arange(rows_here, dtype=jnp.int32))  41.5 us
    gather x16, local copies, waits for them, and re-layouts, step(): remote = extended[columns - first_fine + reach]  39.7 us
    reduce_scatter x1, waiting for transfers between devices, per_device(): total = lax.psum_scatter(received, 'col', scatter_dimension=1, tiled=True)  39.3 us
    gather x32, local copies, waits for them, and re-layouts, step(): coarse_j = p_cols[columns]  35.9 us
    ppermute x2, waiting for transfers between devices, passed_along(): return lax.ppermute(block, axis, route)  27.5 us
    gather x16, local copies, waits for them, and re-layouts, step(): pattern = c_cols[coarse_i]  25.6 us
    dot_general x16, matrix products, step(): jnp.einsum('paxk,aqky->paqxy', left, remote, preferred_element_type=jnp.f...  23.2 us
  transfers between devices with their start and end apart: 5, of which 5 were waited for; matrix products, arithmetic and copies ran while one was open for 1% of the time, Pallas kernels for 0%

commit v1 on v0

v1 whole, which is shorter than its diff:
```python
import functools

import jax
import jax.numpy as jnp
from jax import lax
from jax.experimental import pallas as pl
from jax.experimental.pallas import tpu as pltpu
from jax.sharding import PartitionSpec as P

MESH = pl.DeviceIdType.MESH
BS = 128
RB = 16
KP = 3
KA = 2
KC = 8
HALO = 8
GROUPS = 4
GR = 4
WI = 5
WC = 9
NI = 8
NK = 12
HT = HALO * KP
LT = RB * KP
ZERO_TILE = 2 * HT + LT
F32 = jnp.float32
BF16 = jnp.bfloat16


def select_slot(wanted, columns, values, otherwise):
    picked = jnp.int32(otherwise)
    for column, value in zip(columns, values):
        picked = jnp.where(column == wanted, value, picked)
    return picked


def kernel(
    rows, cols,
    a_cols_ref, p_cols_ref, c_cols_ref, a_ref, p_ref,
    out_ref,
    ac, pc, cc, p_buf, a_buf, left, lhs, rhs, acc, edge_out, edge_in, own, part_out, part_in,
    local_sem, halo_send, halo_recv, edge_send, edge_recv, part_send, part_recv,
):
    r = lax.axis_index("row")
    x = lax.axis_index("col")
    core = lax.rem(r, 2)
    before = lax.rem(r + rows - 1, rows)
    after = lax.rem(r + 1, rows)
    far = jnp.where(core == 0, before, after)
    near = jnp.where(core == 0, after, before)

    local = [
        pltpu.make_async_copy(src, dst, local_sem.at[i])
        for i, (src, dst) in enumerate((
            (p_ref, p_buf.at[pl.ds(HT, LT)]),
            (a_ref, a_buf),
            (a_cols_ref, ac),
            (p_cols_ref, pc),
            (c_cols_ref, cc),
        ))
    ]
    for copy in local:
        copy.start()

    barrier = pltpu.get_barrier_semaphore()
    for target in (before, after):
        pl.semaphore_signal(barrier, inc=1, device_id={"row": target}, device_id_type=MESH)
    for d in range(1, cols):
        pl.semaphore_signal(
            barrier, inc=1, device_id={"col": lax.rem(x + d, cols)}, device_id_type=MESH
        )
    pl.semaphore_wait(barrier, 2 + cols - 1)

    halo = [
        pltpu.make_async_remote_copy(
            src_ref=p_ref.at[pl.ds(src, HT)],
            dst_ref=p_buf.at[pl.ds(dst, HT)],
            send_sem=halo_send.at[i],
            recv_sem=halo_recv.at[i],
            device_id={"row": target},
            device_id_type=MESH,
        )
        for i, (src, dst, target) in enumerate(((0, HT + LT, before), (LT - HT, 0, after)))
    ]
    for copy in halo:
        copy.start()

    p_buf[ZERO_TILE] = jnp.zeros((BS, BS), BF16)

    def clear_acc(k, _):
        acc[k] = jnp.zeros((NI * BS, BS), F32)
        return 0

    lax.fori_loop(0, NK + 1, clear_acc, 0)
    local[0].wait()
    local[1].wait()

    def make_left(g, _):
        tiles = jnp.concatenate([a_buf[g * KA + a] for a in range(KA)], axis=1)
        for p in range(KP):
            left[g * (KP + 1) + p] = lax.dot_general(
                p_buf[HT + g * KP + p], tiles, (((0,), (0,)), ((), ())),
                preferred_element_type=F32,
            ).astype(BF16)
        left[g * (KP + 1) + KP] = jnp.zeros((BS, KA * BS), BF16)
        return 0

    lax.fori_loop(0, RB, make_left, 0)
    for copy in local[2:]:
        copy.wait()

    def make_lhs(gi, _):
        for gg in range(GR):
            g = gi * GR + gg
            columns = [pc[p, r * RB + g] for p in range(KP)]
            for s in range(WI):
                slot = select_slot(r * GROUPS - 2 + gi + s, columns, range(KP), KP)
                lhs[gi, s * BS:(s + 1) * BS, gg * KA * BS:(gg + 1) * KA * BS] = (
                    left[g * (KP + 1) + slot]
                )
        return 0

    lax.fori_loop(0, GROUPS, make_lhs, 0)
    for copy in halo:
        copy.wait()

    def group(t, _):
        gi = jnp.where(core == 0, t, GROUPS - 1 - t)
        for gg in range(GR):
            g = gi * GR + gg
            for a in range(KA):
                j = ac[a, g]
                columns = [pc[q, j] for q in range(KP)]
                first = jnp.clip(j - (r * RB - HALO), 0, RB + 2 * HALO - 1) * KP
                values = [first + q for q in range(KP)]
                for w in range(WC):
                    tile = select_slot(r * GROUPS - 4 + gi + w, columns, values, ZERO_TILE)
                    at = (gg * KA + a) * BS
                    rhs[at:at + BS, w * BS:(w + 1) * BS] = p_buf[tile]
        i_rows = pl.ds(pl.multiple_of(gi * BS, BS), WI * BS)
        for w in range(0, WC, 2):
            wide = min(2, WC - w)
            piece = jnp.dot(
                lhs[gi], rhs[:, w * BS:(w + wide) * BS], preferred_element_type=F32
            )
            for u in range(wide):
                acc[gi + w + u, i_rows, :] += piece[:, u * BS:(u + 1) * BS]
        return 0

    def tile_of(row, s):
        i = r * GROUPS - 2 + row
        i = jnp.clip(i, 0, rows * GROUPS - 1)
        k = cc[s, i] - (r * GROUPS - 4)
        k = jnp.where(jnp.logical_and(k >= 0, k < NK), k, NK)
        return acc[k, pl.ds(pl.multiple_of(row * BS, BS), BS), :]

    def send_edge(side, first_row, target):
        def one(n, _):
            i, s = n // KC, n % KC
            edge_out[side, n] = tile_of(first_row + i, s).astype(BF16)
            return 0

        lax.fori_loop(0, 2 * KC, one, 0)
        copy = pltpu.make_async_remote_copy(
            src_ref=edge_out.at[side],
            dst_ref=edge_in.at[side],
            send_sem=edge_send.at[side],
            recv_sem=edge_recv.at[side],
            device_id={"row": target},
            device_id_type=MESH,
        )
        copy.start()
        return copy

    lax.fori_loop(0, 2, group, 0)
    far_edge = send_edge(0, jnp.where(core == 0, 0, 6), far)
    lax.fori_loop(2, 4, group, 0)
    near_edge = send_edge(1, jnp.where(core == 0, 6, 0), near)

    def send_parts(side, first_row):
        def one(n, _):
            i, s = n // KC, n % KC
            total = tile_of(first_row + i, s) + edge_in[side, n].astype(F32)
            own[side, n] = total
            size = BS // cols
            for part in range(cols):
                part_out[side, part, n] = total[part * size:(part + 1) * size].astype(BF16)
            return 0

        lax.fori_loop(0, 2 * KC, one, 0)
        copies = []
        for d in range(1, cols):
            target = lax.rem(x + d, cols)
            copies.append(pltpu.make_async_remote_copy(
                src_ref=part_out.at[side, target],
                dst_ref=part_in.at[side, d - 1],
                send_sem=part_send.at[side, d - 1],
                recv_sem=part_recv.at[side, d - 1],
                device_id={"col": target},
                device_id_type=MESH,
            ))
            copies[-1].start()
        return copies

    near_row = jnp.where(core == 0, 4, 2)
    far_row = jnp.where(core == 0, 2, 4)
    near_edge.wait()
    near_parts = send_parts(1, near_row)
    far_edge.wait()
    far_parts = send_parts(0, far_row)

    def finish(side, first_row, copies):
        for copy in copies:
            copy.wait()
        size = BS // cols
        mine = pl.ds(pl.multiple_of(x * size, size), size)

        def one(n, _):
            i, s = n // KC, n % KC
            total = own[side, n, mine, :]
            for d in range(cols - 1):
                total = total + part_in[side, d, n].astype(F32)
            out_ref[(first_row - 2 + i) * KC + s] = total
            return 0

        lax.fori_loop(0, 2 * KC, one, 0)

    finish(1, near_row, near_parts)
    finish(0, far_row, far_parts)


def per_device(rows, cols, a_tiles, a_cols, p_tiles, p_cols, c_cols):
    size = BS // cols
    dma = pltpu.SemaphoreType.DMA
    hbm = pl.BlockSpec(memory_space=pl.ANY)
    out = pl.pallas_call(
        functools.partial(kernel, rows, cols),
        out_shape=jax.ShapeDtypeStruct((GROUPS * KC, size, BS), F32),
        in_specs=[hbm] * 5,
        out_specs=pl.BlockSpec(memory_space=pltpu.VMEM),
        scratch_shapes=[
            pltpu.SMEM((KA, RB), jnp.int32),
            pltpu.SMEM(p_cols.shape[::-1], jnp.int32),
            pltpu.SMEM(c_cols.shape[::-1], jnp.int32),
            pltpu.VMEM((ZERO_TILE + 1, BS, BS), BF16),
            pltpu.VMEM((RB * KA, BS, BS), BF16),
            pltpu.VMEM((RB * (KP + 1), BS, KA * BS), BF16),
            pltpu.VMEM((GROUPS, WI * BS, GR * KA * BS), BF16),
            pltpu.VMEM((GR * KA * BS, WC * BS), BF16),
            pltpu.VMEM((NK + 1, NI * BS, BS), F32),
            pltpu.VMEM((2, 2 * KC, BS, BS), BF16),
            pltpu.VMEM((2, 2 * KC, BS, BS), BF16),
            pltpu.VMEM((2, 2 * KC, BS, BS), F32),
            pltpu.VMEM((2, cols, 2 * KC, size, BS), BF16),
            pltpu.VMEM((2, cols - 1, 2 * KC, size, BS), BF16),
            dma((5,)),
            dma((2,)),
            dma((2,)),
            dma((2,)),
            dma((2,)),
            dma((2, cols - 1)),
            dma((2, cols - 1)),
        ],
        compiler_params=pltpu.CompilerParams(
            collective_id=0, has_side_effects=True, vmem_limit_bytes=58 * 1024 * 1024
        ),
    )(
        a_cols.T, p_cols.T, c_cols.T,
        a_tiles.reshape(RB * KA, BS, BS), p_tiles.reshape(LT, BS, BS),
    )
    return out.reshape(GROUPS, KC, size, BS)


def solution(mesh):
    rows, cols = mesh.shape["row"], mesh.shape["col"]
    in_specs = (P("row", "col", None, None), P("row", "col"), P("row", None, None, None), P(), P())
    return jax.shard_map(
        functools.partial(per_device, rows, cols),
        mesh=mesh, in_specs=in_specs, out_specs=P("row", None, "col", None), check_vma=False,
    )
```

time: 460 us -> 60.9 us (0.13)
  the two profiles are of different devices: /device:TPU:24 before, /device:TPU:1 now
where the time goes in v1:
time: 60.9 us; the launch traced here: 60.7 us
  Pallas kernels  58.8 us (97%)
  local copies, waits for them, and re-layouts  1.87 us (3%)
    pallas_call x1, Pallas kernels, per_device(): pl.pallas_call(functools.partial(kernel, rows, cols), out_shape=jax.Shape...  58.8 us
    unnamed x1, local copies, waits for them, and re-layouts  1.87 us

profile of v1, /device:TPU:1, one launch (start us, length us, event | category | flops | bytes accessed | tf_op | source)
XLA Modules:
  0.0 60.7 jit_solution(15775956454388894366)
XLA Ops:
  0.0 58.8 %shard_map.55 = f32[32,32,128]{2,1,0:T(8,128)} custom-call(s32[2,16]{1,0:T(2,128)} %bitcast.11, s32[3,4096]{1,0:T(4,128)} %bitcast.9, s32[8,1024]{1,0:T(8,128)} %bitcast.10, bf16[32,128,128]{2,1,0:T(8,128)(2,1)} %bitcast.8, bf16[48,128,128]{2,1,0:T(8,128)(2,1)} %bitcast.7), custom_call_target="tpu_custom_call" | custom-call | tf_op jit(solution)/shard_map/pallas_call | solution.py:236
  58.8 1.9 %copy.7 = f32[4,8,32,128]{3,2,1,0:T(8,128)} copy(f32[4,8,32,128]{3,2,1,0:T(8,128)} %bitcast.6) | data formatting | bytes 1048576

commit v2 on v1

v2 whole, which is shorter than its diff:
```python
import functools

import jax
import jax.numpy as jnp
from jax import lax
from jax.experimental import pallas as pl
from jax.experimental.pallas import tpu as pltpu
from jax.sharding import PartitionSpec as P

MESH = pl.DeviceIdType.MESH
BS = 128
RB = 16
KP = 3
KA = 2
KC = 8
HALO = 8
GROUPS = 4
GR = 4
WI = 5
WC = 9
NI = 8
NK = 12
HT = HALO * KP
LT = RB * KP
ZERO_TILE = HT + LT
PAIR = 2 * KC
FAR, NEAR = 0, 1
F32 = jnp.float32
BF16 = jnp.bfloat16


def select_slot(wanted, columns, values, otherwise):
    picked = jnp.int32(otherwise)
    for column, value in zip(columns, values):
        picked = jnp.where(column == wanted, value, picked)
    return picked


def tiles_at(first, count):
    return pl.ds(pl.multiple_of(first * BS, BS), count * BS)


def kernel(
    rows, cols,
    a_cols_ref, p_cols_ref, c_cols_ref, a_ref, p_ref,
    out_ref,
    ac, pc, cc, far_buf, near_buf, a_buf, left, lhs, rhs, acc,
    edge_out, edge_in, own, part_out, merged, part_in, relay_in,
    local_sem, near_send, near_recv, far_send, far_recv, hop_send, hop_recv,
    edge_send, edge_recv, part_send, part_recv,
):
    r = lax.axis_index("row")
    x = lax.axis_index("col")
    first_core = lax.rem(r, 2) == 0

    def by_core(zero, one):
        return jnp.where(first_core, zero, one)

    before = lax.rem(r + rows - 1, rows)
    after = lax.rem(r + 1, rows)
    far = by_core(before, after)
    near = by_core(after, before)
    up = lax.rem(x + 1, cols)
    across = lax.rem(x + 2, cols)
    down = lax.rem(x + 3, cols)

    def send(src, dst, sems, recv_sems, at, **device):
        copy = pltpu.make_async_remote_copy(
            src_ref=src, dst_ref=dst, send_sem=sems.at[at], recv_sem=recv_sems.at[at],
            device_id=device, device_id_type=MESH,
        )
        copy.start()
        return copy

    far_rows = by_core(HT, 0)
    near_rows = by_core(0, HT)
    local = [
        pltpu.make_async_copy(src, dst, local_sem.at[i])
        for i, (src, dst) in enumerate((
            (p_ref, near_buf.at[pl.ds(near_rows, LT)]),
            (a_ref, a_buf),
            (a_cols_ref, ac),
            (p_cols_ref, pc),
            (c_cols_ref, cc),
            (p_ref, far_buf.at[pl.ds(far_rows, LT)]),
        ))
    ]
    for copy in local:
        copy.start()

    barrier = pltpu.get_barrier_semaphore()
    for target in (before, after):
        pl.semaphore_signal(barrier, inc=1, device_id={"row": target}, device_id_type=MESH)
    for target in (up, down):
        pl.semaphore_signal(barrier, inc=1, device_id={"col": target}, device_id_type=MESH)
    pl.semaphore_wait(barrier, 4)

    far_src = by_core(0, LT - HT)
    far_there = by_core(LT, 0)
    far_here = by_core(0, LT)
    far_halo = []
    for k, (row, count) in enumerate(((x, 1), (across, 1), (4, 2), (6, 2))):
        far_halo.append(send(
            p_ref.at[pl.ds(far_src + row * KP, count * KP)],
            far_buf.at[pl.ds(far_there + row * KP, count * KP)],
            far_send, far_recv, k, row=far,
        ))
    near_halo = send(
        p_ref.at[pl.ds(by_core(LT - HT, 0), HT)],
        near_buf.at[pl.ds(by_core(0, LT), HT)],
        near_send, near_recv, 0, row=near,
    )

    far_buf[ZERO_TILE] = jnp.zeros((BS, BS), BF16)
    near_buf[ZERO_TILE] = jnp.zeros((BS, BS), BF16)

    def clear_acc(k, _):
        acc[k] = jnp.zeros((NI * BS, BS), F32)
        return 0

    lax.fori_loop(0, NK + 1, clear_acc, 0)
    local[0].wait()
    local[1].wait()

    def make_left(g, _):
        tiles = jnp.concatenate([a_buf[g * KA + a] for a in range(KA)], axis=1)
        interp = jnp.concatenate(
            [near_buf[near_rows + g * KP + p] for p in range(KP)], axis=1
        )
        product = lax.dot_general(
            interp, tiles, (((0,), (0,)), ((), ())), preferred_element_type=F32
        ).astype(BF16)
        for p in range(KP):
            left[g * (KP + 1) + p] = product[p * BS:(p + 1) * BS]
        left[g * (KP + 1) + KP] = jnp.zeros((BS, KA * BS), BF16)
        return 0

    lax.fori_loop(0, 8, make_left, 0, unroll=2)
    far_halo[0].wait_recv()
    here = far_buf.at[pl.ds(far_here + x * KP, KP)]
    hops = [
        send(here, here, hop_send, hop_recv, n, col=target)
        for n, target in enumerate((up, down))
    ]
    lax.fori_loop(8, RB, make_left, 0, unroll=2)
    for copy in local[2:]:
        copy.wait()

    def make_lhs(gi, _):
        for gg in range(GR):
            g = gi * GR + gg
            columns = [pc[p, r * RB + g] for p in range(KP)]
            for s in range(WI):
                slot = select_slot(r * GROUPS - 2 + gi + s, columns, range(KP), KP)
                lhs[gi, s * BS:(s + 1) * BS, gg * KA * BS:(gg + 1) * KA * BS] = (
                    left[g * (KP + 1) + slot]
                )
        return 0

    lax.fori_loop(0, GROUPS, make_lhs, 0)
    def make_rhs(group):
        gi = by_core(group, GROUPS - 1 - group)
        if group < 2:
            buf, first_row = far_buf, r * RB - by_core(HALO, 0)
        else:
            buf, first_row = near_buf, r * RB - by_core(0, HALO)
        for gg in range(GR):
            for a in range(KA):
                j = ac[a, gi * GR + gg]
                columns = [pc[q, j] for q in range(KP)]
                first = jnp.clip(j - first_row, 0, RB + HALO - 1) * KP
                values = [first + q for q in range(KP)]
                at = (gg * KA + a) * BS
                for w in range(WC):
                    tile = select_slot(r * GROUPS - 4 + gi + w, columns, values, ZERO_TILE)
                    rhs[gi, at:at + BS, w * BS:(w + 1) * BS] = buf[tile]

    def add_block(group, row, count):
        gi = by_core(group, GROUPS - 1 - group)
        i = by_core(row, NI - row - count)
        for w in range(0, WC, 2):
            wide = min(2, WC - w)
            piece = jnp.dot(
                lhs[gi, tiles_at(i - gi, count), :], rhs[gi, :, w * BS:(w + wide) * BS],
                preferred_element_type=F32,
            )
            for u in range(wide):
                acc[gi + w + u, tiles_at(i, count), :] += piece[:, u * BS:(u + 1) * BS]

    def tile_of(row, s):
        i = jnp.clip(r * GROUPS - 2 + row, 0, rows * GROUPS - 1)
        k = cc[s, i] - (r * GROUPS - 4)
        k = jnp.where(jnp.logical_and(k >= 0, k < NK), k, NK)
        return acc[k, tiles_at(row, 1), :]

    def send_edge(side, row, order, target):
        i = by_core(row, NI - 1 - row)

        def one(s, _):
            edge_out[side, lax.rem(i, 2) * KC + s] = tile_of(i, s).astype(BF16)
            return 0

        lax.fori_loop(0, KC, one, 0)
        at = pl.ds(lax.rem(i, 2) * KC, KC)
        return send(
            edge_out.at[side, at], edge_in.at[side, at], edge_send, edge_recv,
            2 * side + order, row=target,
        )

    near_halo.wait()
    make_rhs(3)
    add_block(3, 3, 5)
    near_edges = [send_edge(NEAR, 7, 0, near)]
    for copy in far_halo[1:]:
        copy.wait_recv()
    for copy in far_halo:
        copy.wait_send()
    for copy in hops:
        copy.wait()
    make_rhs(0)
    add_block(0, 0, 2)
    far_edges = [send_edge(FAR, 0, 0, far)]
    make_rhs(1)
    add_block(1, 1, 1)
    far_edges.append(send_edge(FAR, 1, 1, far))
    make_rhs(2)
    add_block(2, 2, 5)
    near_edges.append(send_edge(NEAR, 6, 1, near))
    add_block(1, 4, 2)
    add_block(0, 4, 1)

    size = BS // cols

    def part_of(part):
        return pl.ds(pl.multiple_of(part * size, size), size)

    def send_parts(side, first_row):
        def one(n, _):
            total = tile_of(first_row + n // KC, n % KC) + edge_in[side, n].astype(F32)
            own[side, n] = total
            for part in range(cols):
                part_out[side, part, n] = total[part * size:(part + 1) * size].astype(BF16)
            return 0

        lax.fori_loop(0, PAIR, one, 0)
        relays, direct = [], []
        for way, target in enumerate((up, down)):
            first, last = pl.ds(way * KC, KC), pl.ds((1 - way) * KC, KC)
            relays.append(send(
                part_out.at[side, across, first], relay_in.at[side, way],
                part_send, part_recv, 6 * side + 3 * way, col=target,
            ))
            direct.append(send(
                part_out.at[side, target, last], part_in.at[side, way, last],
                part_send, part_recv, 6 * side + 3 * way + 1, col=target,
            ))
        return relays, direct

    def send_merged(side, relays):
        copies = []
        for way, target in enumerate((up, down)):
            relays[way].wait()

            def one(n, _):
                total = own[side, way * KC + n, part_of(target), :]
                merged[side, way, n] = (total + relay_in[side, way, n].astype(F32)).astype(BF16)
                return 0

            lax.fori_loop(0, KC, one, 0)
            copies.append(send(
                merged.at[side, way], part_in.at[side, way, pl.ds(way * KC, KC)],
                part_send, part_recv, 6 * side + 3 * way + 2, col=target,
            ))
        return copies

    def finish(side, first_row, copies):
        for copy in copies:
            copy.wait()

        def one(n, _):
            total = own[side, n, part_of(x), :]
            for way in range(2):
                total = total + part_in[side, way, n].astype(F32)
            out_ref[(first_row - 2) * KC + n] = total
            return 0

        lax.fori_loop(0, PAIR, one, 0)

    near_row = by_core(4, 2)
    far_row = by_core(2, 4)
    for copy in near_edges:
        copy.wait()
    near_relays, near_direct = send_parts(NEAR, near_row)
    for group, row, count in ((0, 2, 2), (1, 2, 2)):
        add_block(group, row, count)
    near_merged = send_merged(NEAR, near_relays)
    for copy in far_edges:
        copy.wait()
    far_relays, far_direct = send_parts(FAR, far_row)
    far_merged = send_merged(FAR, far_relays)
    finish(NEAR, near_row, near_direct + near_merged)
    finish(FAR, far_row, far_direct + far_merged)


def per_device(rows, cols, a_tiles, a_cols, p_tiles, p_cols, c_cols):
    size = BS // cols
    dma = pltpu.SemaphoreType.DMA
    hbm = pl.BlockSpec(memory_space=pl.ANY)
    out = pl.pallas_call(
        functools.partial(kernel, rows, cols),
        out_shape=pltpu.VMEM((GROUPS * KC, size, BS), F32),
        in_specs=[hbm] * 5,
        out_specs=pl.BlockSpec(memory_space=pltpu.VMEM),
        scratch_shapes=[
            pltpu.SMEM((KA, RB), jnp.int32),
            pltpu.SMEM(p_cols.shape[::-1], jnp.int32),
            pltpu.SMEM(c_cols.shape[::-1], jnp.int32),
            pltpu.VMEM((ZERO_TILE + 1, BS, BS), BF16),
            pltpu.VMEM((ZERO_TILE + 1, BS, BS), BF16),
            pltpu.VMEM((RB * KA, BS, BS), BF16),
            pltpu.VMEM((RB * (KP + 1), BS, KA * BS), BF16),
            pltpu.VMEM((GROUPS, WI * BS, GR * KA * BS), BF16),
            pltpu.VMEM((GROUPS, GR * KA * BS, WC * BS), BF16),
            pltpu.VMEM((NK + 1, NI * BS, BS), F32),
            pltpu.VMEM((2, PAIR, BS, BS), BF16),
            pltpu.VMEM((2, PAIR, BS, BS), BF16),
            pltpu.VMEM((2, PAIR, BS, BS), F32),
            pltpu.VMEM((2, cols, PAIR, size, BS), BF16),
            pltpu.VMEM((2, 2, KC, size, BS), BF16),
            pltpu.VMEM((2, 2, PAIR, size, BS), BF16),
            pltpu.VMEM((2, 2, KC, size, BS), BF16),
            dma((6,)),
            dma((1,)),
            dma((1,)),
            dma((4,)),
            dma((4,)),
            dma((2,)),
            dma((2,)),
            dma((4,)),
            dma((4,)),
            dma((12,)),
            dma((12,)),
        ],
        compiler_params=pltpu.CompilerParams(
            collective_id=0, has_side_effects=True, vmem_limit_bytes=58 * 1024 * 1024
        ),
    )(
        a_cols.T, p_cols.T, c_cols.T,
        a_tiles.reshape(RB * KA, BS, BS), p_tiles.reshape(LT, BS, BS),
    )
    return out.reshape(GROUPS, KC, size, BS)


def solution(mesh):
    rows, cols = mesh.shape["row"], mesh.shape["col"]
    in_specs = (P("row", "col", None, None), P("row", "col"), P("row", None, None, None), P(), P())
    return jax.shard_map(
        functools.partial(per_device, rows, cols),
        mesh=mesh, in_specs=in_specs, out_specs=P("row", None, "col", None), check_vma=False,
    )
```

time: 60.9 us -> 50.5 us (0.83)
  the two profiles are of different devices: /device:TPU:1 before, /device:TPU:6 now
where the time goes in v2:
time: 50.5 us; the launch traced here: 50.4 us
  Pallas kernels  49.6 us (98%)
  local copies, waits for them, and re-layouts  0.8 us (2%)
    pallas_call x1, Pallas kernels, per_device(): pl.pallas_call(functools.partial(kernel, rows, cols), out_shape=pltpu.VME...  49.6 us

profile of v2, /device:TPU:6, one launch (start us, length us, event | category | flops | bytes accessed | tf_op | source)
XLA Modules:
  0.0 50.4 jit_solution(6667011631512409829)
XLA Ops:
  0.0 49.6 %shard_map.55 = f32[32,32,128]{2,1,0:T(8,128)S(1)} custom-call(s32[2,16]{1,0:T(2,128)} %bitcast.11, s32[3,4096]{1,0:T(4,128)} %bitcast.9, s32[8,1024]{1,0:T(8,128)} %bitcast.10, bf16[32,128,128]{2,1,0:T(8,128)(2,1)} %bitcast.8, bf16[48,128,128]{2,1,0:T(8,128)(2,1)} %bitcast.7), custom_call_target="tpu_custom_call" | custom-call | tf_op jit(solution)/shard_map/pallas_call | solution.py:309
  49.6 0.8 %copy.7 = f32[4,8,32,128]{3,2,1,0:T(8,128)} copy(f32[4,8,32,128]{3,2,1,0:T(8,128)S(1)} %bitcast.6) | data formatting | bytes 1048576

commit v3 on v2

--- a/solution.py
+++ b/solution.py
@@ -99,10 +99,11 @@
     far_there = by_core(LT, 0)
     far_here = by_core(0, LT)
     far_halo = []
-    for k, (row, count) in enumerate(((x, 1), (across, 1), (4, 2), (6, 2))):
+    for k, (tile, count) in enumerate((
+        (4 * x, 2), (4 * x + 2, 2), (4 * across, 4), (16, 4), (20, 4)
+    )):
         far_halo.append(send(
-            p_ref.at[pl.ds(far_src + row * KP, count * KP)],
-            far_buf.at[pl.ds(far_there + row * KP, count * KP)],
+            p_ref.at[pl.ds(far_src + tile, count)], far_buf.at[pl.ds(far_there + tile, count)],
             far_send, far_recv, k, row=far,
         ))
     near_halo = send(
@@ -135,14 +136,16 @@
         left[g * (KP + 1) + KP] = jnp.zeros((BS, KA * BS), BF16)
         return 0
 
-    lax.fori_loop(0, 8, make_left, 0, unroll=2)
-    far_halo[0].wait_recv()
-    here = far_buf.at[pl.ds(far_here + x * KP, KP)]
-    hops = [
-        send(here, here, hop_send, hop_recv, n, col=target)
-        for n, target in enumerate((up, down))
-    ]
-    lax.fori_loop(8, RB, make_left, 0, unroll=2)
+    hops = []
+
+    def forward(k):
+        far_halo[k].wait_recv()
+        here = far_buf.at[pl.ds(far_here + 4 * x + 2 * k, 2)]
+        for n, target in enumerate((up, down)):
+            hops.append(send(here, here, hop_send, hop_recv, 2 * k + n, col=target))
+
+    lax.fori_loop(0, RB, make_left, 0, unroll=2)
+    forward(0)
     for copy in local[2:]:
         copy.wait()
 
@@ -158,6 +161,7 @@
         return 0
 
     lax.fori_loop(0, GROUPS, make_lhs, 0)
+    forward(1)
     def make_rhs(group):
         gi = by_core(group, GROUPS - 1 - group)
         if group < 2:
@@ -193,113 +197,146 @@
         k = jnp.where(jnp.logical_and(k >= 0, k < NK), k, NK)
         return acc[k, tiles_at(row, 1), :]
 
-    def send_edge(side, row, order, target):
+    def send_edge(side, row, first, count, order, target):
         i = by_core(row, NI - 1 - row)
+        slot = lax.rem(i, 2) * KC + first
 
         def one(s, _):
-            edge_out[side, lax.rem(i, 2) * KC + s] = tile_of(i, s).astype(BF16)
+            edge_out[side, slot + s] = tile_of(i, first + s).astype(BF16)
             return 0
 
-        lax.fori_loop(0, KC, one, 0)
-        at = pl.ds(lax.rem(i, 2) * KC, KC)
+        lax.fori_loop(0, count, one, 0, unroll=4)
+        at = pl.ds(slot, count)
         return send(
             edge_out.at[side, at], edge_in.at[side, at], edge_send, edge_recv,
-            2 * side + order, row=target,
+            order, row=target,
         )
 
     near_halo.wait()
     make_rhs(3)
     add_block(3, 3, 5)
-    near_edges = [send_edge(NEAR, 7, 0, near)]
-    for copy in far_halo[1:]:
+    near_edges = [send_edge(NEAR, 7, 0, KC, 0, near)]
+    make_rhs(2)
+    add_block(2, 2, 5)
+    near_edges.append(send_edge(NEAR, 6, 0, KC, 1, near))
+    for copy in far_halo[2:]:
         copy.wait_recv()
-    for copy in far_halo:
-        copy.wait_send()
     for copy in hops:
         copy.wait()
-    make_rhs(0)
-    add_block(0, 0, 2)
-    far_edges = [send_edge(FAR, 0, 0, far)]
-    make_rhs(1)
-    add_block(1, 1, 1)
-    far_edges.append(send_edge(FAR, 1, 1, far))
-    make_rhs(2)
-    add_block(2, 2, 5)
-    near_edges.append(send_edge(NEAR, 6, 1, near))
-    add_block(1, 4, 2)
-    add_block(0, 4, 1)
-
     size = BS // cols
+    half = KC // 2
 
     def part_of(part):
         return pl.ds(pl.multiple_of(part * size, size), size)
 
-    def send_parts(side, first_row):
-        def one(n, _):
-            total = tile_of(first_row + n // KC, n % KC) + edge_in[side, n].astype(F32)
-            own[side, n] = total
+    def make_parts(order, side, row, first, count):
+        i = by_core(row, NI - 1 - row)
+        slot = lax.rem(i, 2) * KC
+
+        def one(s, _):
+            total = tile_of(i, s) + edge_in[side, slot + s].astype(F32)
+            own[order, s] = total
             for part in range(cols):
-                part_out[side, part, n] = total[part * size:(part + 1) * size].astype(BF16)
+                part_out[order, part, s] = total[part * size:(part + 1) * size].astype(BF16)
             return 0
 
-        lax.fori_loop(0, PAIR, one, 0)
+        lax.fori_loop(first, first + count, one, 0, unroll=4)
+
+    def send_part(src, dst, order, at, target):
+        return send(src, dst, part_send, part_recv, order * 6 + at, col=target)
+
+    def send_halves(order):
         relays, direct = [], []
         for way, target in enumerate((up, down)):
-            first, last = pl.ds(way * KC, KC), pl.ds((1 - way) * KC, KC)
-            relays.append(send(
-                part_out.at[side, across, first], relay_in.at[side, way],
-                part_send, part_recv, 6 * side + 3 * way, col=target,
+            first, last = pl.ds(way * half, half), pl.ds((1 - way) * half, half)
+            relays.append(send_part(
+                part_out.at[order, across, first], relay_in.at[order, way], order, way, target
             ))
-            direct.append(send(
-                part_out.at[side, target, last], part_in.at[side, way, last],
-                part_send, part_recv, 6 * side + 3 * way + 1, col=target,
+            direct.append(send_part(
+                part_out.at[order, target, last], part_in.at[order, way, last],
+                order, 2 + way, target,
             ))
         return relays, direct
 
-    def send_merged(side, relays):
+    def send_merged(order, relays):
         copies = []
         for way, target in enumerate((up, down)):
             relays[way].wait()
 
             def one(n, _):
-                total = own[side, way * KC + n, part_of(target), :]
-                merged[side, way, n] = (total + relay_in[side, way, n].astype(F32)).astype(BF16)
+                total = own[order, way * half + n, part_of(target), :]
+                merged[order, way, n] = (
+                    total + relay_in[order, way, n].astype(F32)
+                ).astype(BF16)
                 return 0
 
-            lax.fori_loop(0, KC, one, 0)
-            copies.append(send(
-                merged.at[side, way], part_in.at[side, way, pl.ds(way * KC, KC)],
-                part_send, part_recv, 6 * side + 3 * way + 2, col=target,
+            lax.fori_loop(0, half, one, 0, unroll=4)
+            copies.append(send_part(
+                merged.at[order, way], part_in.at[order, way, pl.ds(way * half, half)],
+                order, 4 + way, target,
             ))
         return copies
 
-    def finish(side, first_row, copies):
+    def send_whole(order, first, count, base):
+        some = pl.ds(first, count)
+        return [
+            send_part(
+                part_out.at[order, target, some], part_in.at[order, at, some],
+                order, base + at, target,
+            )
+            for at, target in ((2, across), (0, up), (1, down))
+        ]
+
+    def finish(order, row, first, count, arrivals, copies):
         for copy in copies:
             copy.wait()
-
-        def one(n, _):
-            total = own[side, n, part_of(x), :]
-            for way in range(2):
-                total = total + part_in[side, way, n].astype(F32)
-            out_ref[(first_row - 2) * KC + n] = total
+        i = by_core(row, NI - 1 - row)
+
+        def one(s, _):
+            total = own[order, s, part_of(x), :]
+            for at in range(arrivals):
+                total = total + part_in[order, at, s].astype(F32)
+            out_ref[(i - 2) * KC + s] = total
             return 0
 
-        lax.fori_loop(0, PAIR, one, 0)
-
-    near_row = by_core(4, 2)
-    far_row = by_core(2, 4)
+        lax.fori_loop(first, first + count, one, 0, unroll=4)
+
+    make_rhs(0)
+    add_block(0, 0, 1)
+    far_edges = [send_edge(FAR, 0, 0, KC, 2, far)]
+    make_rhs(1)
+    add_block(1, 4, 2)
     for copy in near_edges:
         copy.wait()
-    near_relays, near_direct = send_parts(NEAR, near_row)
-    for group, row, count in ((0, 2, 2), (1, 2, 2)):
-        add_block(group, row, count)
-    near_merged = send_merged(NEAR, near_relays)
-    for copy in far_edges:
-        copy.wait()
-    far_relays, far_direct = send_parts(FAR, far_row)
-    far_merged = send_merged(FAR, far_relays)
-    finish(NEAR, near_row, near_direct + near_merged)
-    finish(FAR, far_row, far_direct + far_merged)
+    make_parts(0, NEAR, 5, 0, KC)
+    relays0, direct0 = send_halves(0)
+    add_block(0, 1, 1)
+    add_block(1, 1, 1)
+    for n in range(2):
+        far_edges.append(send_edge(FAR, 1, n * half, half, 3 + n, far))
+    add_block(0, 4, 1)
+    make_parts(1, NEAR, 4, 0, KC)
+    relays1, direct1 = send_halves(1)
+    add_block(0, 2, 2)
+    add_block(1, 2, 2)
+    merged0 = send_merged(0, relays0)
+    far_edges[0].wait()
+    make_parts(2, FAR, 3, 0, KC)
+    relays2, direct2 = send_halves(2)
+    merged1 = send_merged(1, relays1)
+    whole3 = []
+    for n in range(2):
+        far_edges[1 + n].wait()
+        make_parts(3, FAR, 2, n * half, half)
+        whole3.append(send_whole(3, n * half, half, 3 * n))
+    merged2 = send_merged(2, relays2)
+    finish(0, 5, 0, KC, 2, direct0 + merged0)
+    finish(1, 4, 0, KC, 2, direct1 + merged1)
+    finish(2, 3, 0, KC, 2, direct2 + merged2)
+    for n in range(2):
+        finish(3, 2, n * half, half, 3, whole3[n])
+    for copy in far_halo:
+        copy.wait_send()
 
 
 def per_device(rows, cols, a_tiles, a_cols, p_tiles, p_cols, c_cols):
@@ -324,22 +361,22 @@
             pltpu.VMEM((NK + 1, NI * BS, BS), F32),
             pltpu.VMEM((2, PAIR, BS, BS), BF16),
             pltpu.VMEM((2, PAIR, BS, BS), BF16),
-            pltpu.VMEM((2, PAIR, BS, BS), F32),
-            pltpu.VMEM((2, cols, PAIR, size, BS), BF16),
-            pltpu.VMEM((2, 2, KC, size, BS), BF16),
-            pltpu.VMEM((2, 2, PAIR, size, BS), BF16),
-            pltpu.VMEM((2, 2, KC, size, BS), BF16),
+            pltpu.VMEM((4, KC, BS, BS), F32),
+            pltpu.VMEM((4, cols, KC, size, BS), BF16),
+            pltpu.VMEM((4, 2, KC // 2, size, BS), BF16),
+            pltpu.VMEM((4, cols - 1, KC, size, BS), BF16),
+            pltpu.VMEM((4, 2, KC // 2, size, BS), BF16),
             dma((6,)),
             dma((1,)),
             dma((1,)),
+            dma((5,)),
+            dma((5,)),
             dma((4,)),
             dma((4,)),
-            dma((2,)),
-            dma((2,)),
-            dma((4,)),
-            dma((4,)),
-            dma((12,)),
-            dma((12,)),
+            dma((5,)),
+            dma((5,)),
+            dma((24,)),
+            dma((24,)),
         ],
         compiler_params=pltpu.CompilerParams(
             collective_id=0, has_side_effects=True, vmem_limit_bytes=58 * 1024 * 1024

time: 50.5 us -> 45.8 us (0.907)
  the two profiles are of different devices: /device:TPU:6 before, /device:TPU:2 now
where the time goes in v3:
time: 45.8 us; the launch traced here: 45.7 us
  Pallas kernels  44.9 us (98%)
  local copies, waits for them, and re-layouts  0.8 us (2%)
    pallas_call x1, Pallas kernels, per_device(): pl.pallas_call(functools.partial(kernel, rows, cols), out_shape=pltpu.VME...  44.9 us

profile of v3, /device:TPU:2, one launch (start us, length us, event | category | flops | bytes accessed | tf_op | source)
XLA Modules:
  0.0 45.7 jit_solution(14891401516249316912)
XLA Ops:
  0.0 44.9 %shard_map.55 = f32[32,32,128]{2,1,0:T(8,128)S(1)} custom-call(s32[2,16]{1,0:T(2,128)} %bitcast.11, s32[3,4096]{1,0:T(4,128)} %bitcast.9, s32[8,1024]{1,0:T(8,128)} %bitcast.10, bf16[32,128,128]{2,1,0:T(8,128)(2,1)} %bitcast.8, bf16[48,128,128]{2,1,0:T(8,128)(2,1)} %bitcast.7), custom_call_target="tpu_custom_call" | custom-call | tf_op jit(solution)/shard_map/pallas_call | solution.py:346
  44.9 0.8 %copy.7 = f32[4,8,32,128]{3,2,1,0:T(8,128)} copy(f32[4,8,32,128]{3,2,1,0:T(8,128)S(1)} %bitcast.6) | data formatting | bytes 1048576

commit v4 on v3

--- a/solution.py
+++ b/solution.py
@@ -36,6 +36,23 @@
     return picked
 
 
+class Guarded:
+    def __init__(self, copy, made):
+        self.copy, self.made = copy, made
+
+    def start(self):
+        pl.when(self.made)(self.copy.start)
+
+    def wait(self):
+        pl.when(self.made)(self.copy.wait)
+
+    def wait_recv(self):
+        pl.when(self.made)(self.copy.wait_recv)
+
+    def wait_send(self):
+        pl.when(self.made)(self.copy.wait_send)
+
+
 def tiles_at(first, count):
     return pl.ds(pl.multiple_of(first * BS, BS), count * BS)
 
@@ -64,11 +81,15 @@
     across = lax.rem(x + 2, cols)
     down = lax.rem(x + 3, cols)
 
-    def send(src, dst, sems, recv_sems, at, **device):
+    has_far = by_core(r, rows - 1 - r) > 0
+
+    def send(src, dst, sems, recv_sems, at, made=None, **device):
         copy = pltpu.make_async_remote_copy(
             src_ref=src, dst_ref=dst, send_sem=sems.at[at], recv_sem=recv_sems.at[at],
             device_id=device, device_id_type=MESH,
         )
+        if made is not None:
+            copy = Guarded(copy, made)
         copy.start()
         return copy
 
@@ -89,11 +110,15 @@
         copy.start()
 
     barrier = pltpu.get_barrier_semaphore()
-    for target in (before, after):
-        pl.semaphore_signal(barrier, inc=1, device_id={"row": target}, device_id_type=MESH)
+
+    @pl.when(has_far)
+    def _():
+        pl.semaphore_signal(barrier, inc=1, device_id={"row": far}, device_id_type=MESH)
+
+    pl.semaphore_signal(barrier, inc=1, device_id={"row": near}, device_id_type=MESH)
     for target in (up, down):
         pl.semaphore_signal(barrier, inc=1, device_id={"col": target}, device_id_type=MESH)
-    pl.semaphore_wait(barrier, 4)
+    pl.semaphore_wait(barrier, jnp.where(has_far, 4, 3))
 
     far_src = by_core(0, LT - HT)
     far_there = by_core(LT, 0)
@@ -104,13 +129,17 @@
     )):
         far_halo.append(send(
             p_ref.at[pl.ds(far_src + tile, count)], far_buf.at[pl.ds(far_there + tile, count)],
-            far_send, far_recv, k, row=far,
+            far_send, far_recv, k, made=has_far, row=far,
         ))
     near_halo = send(
         p_ref.at[pl.ds(by_core(LT - HT, 0), HT)],
         near_buf.at[pl.ds(by_core(0, LT), HT)],
         near_send, near_recv, 0, row=near,
     )
+
+    @pl.when(jnp.logical_not(has_far))
+    def _():
+        edge_in[FAR] = jnp.zeros((PAIR, BS, BS), BF16)
 
     far_buf[ZERO_TILE] = jnp.zeros((BS, BS), BF16)
     near_buf[ZERO_TILE] = jnp.zeros((BS, BS), BF16)
@@ -142,7 +171,9 @@
         far_halo[k].wait_recv()
         here = far_buf.at[pl.ds(far_here + 4 * x + 2 * k, 2)]
         for n, target in enumerate((up, down)):
-            hops.append(send(here, here, hop_send, hop_recv, 2 * k + n, col=target))
+            hops.append(
+                send(here, here, hop_send, hop_recv, 2 * k + n, made=has_far, col=target)
+            )
 
     lax.fori_loop(0, RB, make_left, 0, unroll=2)
     forward(0)
@@ -209,7 +240,7 @@
         at = pl.ds(slot, count)
         return send(
             edge_out.at[side, at], edge_in.at[side, at], edge_send, edge_recv,
-            order, row=target,
+            order, made=has_far if side == FAR else None, row=target,
         )
 
     near_halo.wait()
@@ -217,7 +248,7 @@
     add_block(3, 3, 5)
     near_edges = [send_edge(NEAR, 7, 0, KC, 0, near)]
     make_rhs(2)
-    add_block(2, 2, 5)
+    add_block(2, 4, 3)
     near_edges.append(send_edge(NEAR, 6, 0, KC, 1, near))
     for copy in far_halo[2:]:
         copy.wait_recv()
@@ -317,6 +348,7 @@
     add_block(0, 4, 1)
     make_parts(1, NEAR, 4, 0, KC)
     relays1, direct1 = send_halves(1)
+    add_block(2, 2, 2)
     add_block(0, 2, 2)
     add_block(1, 2, 2)
     merged0 = send_merged(0, relays0)

time: 45.8 us -> 43.1 us (0.941)
  the two profiles are of different devices: /device:TPU:2 before, /device:TPU:24 now
where the time goes in v4:
time: 43.1 us; the launch traced here: 43 us
  Pallas kernels  42.2 us (98%)
  local copies, waits for them, and re-layouts  0.8 us (2%)
    pallas_call x1, Pallas kernels, per_device(): pl.pallas_call(functools.partial(kernel, rows, cols), out_shape=pltpu.VME...  42.2 us

profile of v4, /device:TPU:24, one launch (start us, length us, event | category | flops | bytes accessed | tf_op | source)
XLA Modules:
  0.0 43.0 jit_solution(6300194336617920907)
XLA Ops:
  0.0 42.2 %shard_map.55 = f32[32,32,128]{2,1,0:T(8,128)S(1)} custom-call(s32[2,16]{1,0:T(2,128)} %bitcast.11, s32[3,4096]{1,0:T(4,128)} %bitcast.9, s32[8,1024]{1,0:T(8,128)} %bitcast.10, bf16[32,128,128]{2,1,0:T(8,128)(2,1)} %bitcast.8, bf16[48,128,128]{2,1,0:T(8,128)(2,1)} %bitcast.7), custom_call_target="tpu_custom_call" | custom-call | tf_op jit(solution)/shard_map/pallas_call | solution.py:378
  42.2 0.8 %copy.7 = f32[4,8,32,128]{3,2,1,0:T(8,128)} copy(f32[4,8,32,128]{3,2,1,0:T(8,128)S(1)} %bitcast.6) | data formatting | bytes 1048576

commit v5 on v4

--- a/solution.py
+++ b/solution.py
@@ -106,7 +106,7 @@
             (p_ref, far_buf.at[pl.ds(far_rows, LT)]),
         ))
     ]
-    for copy in local:
+    for copy in local[:5]:
         copy.start()
 
     barrier = pltpu.get_barrier_semaphore()
@@ -136,6 +136,8 @@
         near_buf.at[pl.ds(by_core(0, LT), HT)],
         near_send, near_recv, 0, row=near,
     )
+
+    local[5].start()
 
     @pl.when(jnp.logical_not(has_far))
     def _():
@@ -348,9 +350,9 @@
     add_block(0, 4, 1)
     make_parts(1, NEAR, 4, 0, KC)
     relays1, direct1 = send_halves(1)
-    add_block(2, 2, 2)
     add_block(0, 2, 2)
     add_block(1, 2, 2)
+    add_block(2, 2, 2)
     merged0 = send_merged(0, relays0)
     far_edges[0].wait()
     make_parts(2, FAR, 3, 0, KC)

time: 43.1 us -> 43.1 us (level)
  no operation moved by 1% of the time
where the time goes in v5:
time: 43.1 us; the launch traced here: 43 us
  Pallas kernels  42.2 us (98%)
  local copies, waits for them, and re-layouts  0.8 us (2%)
    pallas_call x1, Pallas kernels, per_device(): pl.pallas_call(functools.partial(kernel, rows, cols), out_shape=pltpu.VME...  42.2 us

profile of v5, /device:TPU:24, one launch (start us, length us, event | category | flops | bytes accessed | tf_op | source)
XLA Modules:
  0.0 43.0 jit_solution(13646811804929093250)
XLA Ops:
  0.0 42.2 %shard_map.55 = f32[32,32,128]{2,1,0:T(8,128)S(1)} custom-call(s32[2,16]{1,0:T(2,128)} %bitcast.11, s32[3,4096]{1,0:T(4,128)} %bitcast.9, s32[8,1024]{1,0:T(8,128)} %bitcast.10, bf16[32,128,128]{2,1,0:T(8,128)(2,1)} %bitcast.8, bf16[48,128,128]{2,1,0:T(8,128)(2,1)} %bitcast.7), custom_call_target="tpu_custom_call" | custom-call | tf_op jit(solution)/shard_map/pallas_call | solution.py:380
  42.2 0.8 %copy.7 = f32[4,8,32,128]{3,2,1,0:T(8,128)} copy(f32[4,8,32,128]{3,2,1,0:T(8,128)S(1)} %bitcast.6) | data formatting | bytes 1048576
